TPU v7x, 512 devices: a whole 4x4x16 slice. The times are simulated.
512 devices in a mesh: dp: 32 (over z, core), fsdp: 16 (over y, x).
Axes of the slice: x: 4, y: 4, z: 16, core: 2. Of those that a mesh axis runs over, the one named last changes fastest.
Arguments:
- inputs: bfloat16 [12288, 8192], P('dp', 'fsdp'), may hold values from -6 to 6
- out_grad: bfloat16 [12288, 4096], P('dp', 'fsdp'), may hold values from -6 to 6
- base_weight: bfloat16 [8192, 4096], P('fsdp', 'dp'), may hold values from -0.125 to 0.125
- down_maps: bfloat16 [64, 64, 8192], P('dp', None, 'fsdp'), may hold values from -0.0625 to 0.0625
- up_maps: bfloat16 [64, 64, 4096], P('dp', None, 'fsdp'), may hold values from -0.75 to 0.75
- mean_down: float32 [64, 64, 8192], P('dp', None, 'fsdp'), may hold values from -0.5 to 0.5
- square_down: float32 [64, 64, 8192], P('dp', None, 'fsdp'), may hold values from 0.25 to 1.25
- mean_up: float32 [64, 64, 4096], P('dp', None, 'fsdp'), may hold values from -0.5 to 0.5
- square_up: float32 [64, 64, 4096], P('dp', None, 'fsdp'), may hold values from 0.25 to 1.25
- block_member: int32 [1536], P('dp'), may hold values from 0 to 63, as said below
- member_slot: int32 [64], replicated, may hold values from 0 to 63, as said below
Outputs:
- projected: bfloat16 [12288, 4096], P('dp', 'fsdp')
- new_mean_down: float32 [64, 64, 8192], P('dp', None, 'fsdp')
- new_square_down: float32 [64, 64, 8192], P('dp', None, 'fsdp')
- new_mean_up: float32 [64, 64, 4096], P('dp', None, 'fsdp')
- new_square_up: float32 [64, 64, 4096], P('dp', None, 'fsdp')
Inputs may be any that keep to these rules, and one draw needn't show every extreme that they name: `block_member`: of the 48 blocks of one dp index, at most 3 have members whose slots lie with one dp index; in every draw some dp index receives exactly 3 blocks from every dp index. `member_slot`: A permutation: every slot once. Slot s lies with dp index s // 2.
All inputs are finite; a program needn't handle non-finite values.
Results may differ from a plain program's by a relative error of at most 0.022.
Values may be sent and summed in bfloat16 or wider, within the bound.
A program may use at most 64 MiB of HBM per device.

v0:
```python
import jax
import jax.numpy as jnp
from jax import lax
from jax.sharding import PartitionSpec as P

SNAPS = 2


adapter_scale = 2.0
rate_down = 0.002
rate_up = 0.02
contract_last = (((1,), (1,)), ((), ()))
contract_first = (((0,), (0,)), ((), ()))


def body(
    inputs,
    out_grad,
    base_weight,
    down_maps,
    up_maps,
    mean_down,
    square_down,
    mean_up,
    square_up,
    block_member,
    member_slot,
):
    row_count, slab_width = inputs.shape
    out_width = out_grad.shape[1]
    dp_count = lax.axis_size("dp")
    owned_count = down_maps.shape[0]
    rank_width = down_maps.shape[1]
    block_count = block_member.shape[0]
    block_rows = row_count // block_count
    capacity = 2 * block_count // dp_count
    slot_total = dp_count * capacity
    recv_rows = slot_total * block_rows
    member_count = member_slot.shape[0]
    member_ids = jnp.arange(member_count, dtype=jnp.int32)
    block_slot = jnp.sum(
        jnp.where(block_member[:, None] == member_ids[None, :], member_slot[None, :], 0), axis=1
    )
    block_owner = block_slot // owned_count
    block_local = block_slot % owned_count
    block_ids = jnp.arange(block_count, dtype=jnp.int32)
    earlier = (block_owner[None, :] == block_owner[:, None]) & (
        block_ids[None, :] < block_ids[:, None]
    )
    position = jnp.sum(earlier.astype(jnp.int32), axis=1)
    target = block_owner * capacity + position
    dispatch = (target[None, :] == jnp.arange(slot_total, dtype=jnp.int32)[:, None]).astype(
        jnp.bfloat16
    )
    sent_inputs = jnp.dot(
        dispatch,
        inputs.reshape(block_count, block_rows * slab_width),
        preferred_element_type=jnp.float32,
    ).astype(jnp.bfloat16)
    sent_grads = jnp.dot(
        dispatch,
        out_grad.reshape(block_count, block_rows * out_width),
        preferred_element_type=jnp.float32,
    ).astype(jnp.bfloat16)
    slot_tags = jnp.dot(
        dispatch, (block_local + 1).astype(jnp.bfloat16), preferred_element_type=jnp.float32
    )
    row_tags = jnp.broadcast_to(slot_tags[:, None], (slot_total, block_rows)).astype(jnp.bfloat16)
    got_inputs, got_grads, got_tags = (
        lax.all_to_all(
            sent_inputs.reshape(dp_count, capacity * block_rows, slab_width),
            "dp",
            split_axis=0,
            concat_axis=0,
            tiled=True,
        ),
        lax.all_to_all(
            sent_grads.reshape(dp_count, capacity * block_rows, out_width),
            "dp",
            split_axis=0,
            concat_axis=0,
            tiled=True,
        ),
        lax.all_to_all(
            row_tags.reshape(dp_count, capacity * block_rows),
            "dp",
            split_axis=0,
            concat_axis=0,
            tiled=True,
        ),
    )
    partial_value = jnp.dot(
        inputs,
        lax.all_gather(base_weight, "dp", axis=1, tiled=True),
        preferred_element_type=jnp.float32,
    )
    summed = lax.psum(partial_value.astype(jnp.bfloat16), "fsdp").astype(jnp.float32)
    column_sum = lax.dynamic_slice_in_dim(summed, lax.axis_index("fsdp") * out_width, out_width, 1)
    owner_inputs = got_inputs.reshape(recv_rows, slab_width)
    owner_grads = got_grads.reshape(recv_rows, out_width)
    down_stack = down_maps.reshape(owned_count * rank_width, slab_width)
    stacked_up_weight = up_maps.reshape(owned_count * rank_width, out_width)
    down_part = lax.dot_general(
        owner_inputs, down_stack, contract_last, preferred_element_type=jnp.float32
    )
    up_part = lax.dot_general(
        owner_grads, stacked_up_weight, contract_last, preferred_element_type=jnp.float32
    )
    column_owner = (jnp.arange(owned_count * rank_width, dtype=jnp.int32) // rank_width + 1).astype(
        jnp.float32
    )
    member_mask = got_tags.reshape(recv_rows).astype(jnp.float32)[:, None] == column_owner[None, :]
    down_sum, up_sum = (
        lax.psum(down_part.astype(jnp.bfloat16), "fsdp").astype(jnp.float32),
        lax.psum(up_part.astype(jnp.bfloat16), "fsdp").astype(jnp.float32),
    )
    low_rank_product = jnp.where(member_mask, down_sum, 0.0).astype(jnp.bfloat16)
    backward_low_rank = jnp.where(member_mask, up_sum, 0.0).astype(jnp.bfloat16)
    adapted_output = (
        adapter_scale
        * jnp.dot(low_rank_product, stacked_up_weight, preferred_element_type=jnp.float32)
    ).astype(jnp.bfloat16)
    returned = lax.all_to_all(
        adapted_output.reshape(dp_count, capacity * block_rows, out_width),
        "dp",
        split_axis=0,
        concat_axis=0,
        tiled=True,
    )
    up_gradient = adapter_scale * lax.dot_general(
        low_rank_product, owner_grads, contract_first, preferred_element_type=jnp.float32
    )
    down_gradient = adapter_scale * lax.dot_general(
        backward_low_rank, owner_inputs, contract_first, preferred_element_type=jnp.float32
    )
    own_adapted = lax.dot_general(
        dispatch,
        returned.reshape(slot_total, block_rows * out_width),
        contract_first,
        preferred_element_type=jnp.float32,
    )
    projected = (column_sum + own_adapted.reshape(row_count, out_width)).astype(jnp.bfloat16)
    theta_down = down_maps.astype(jnp.float32) - rate_down * down_gradient.reshape(
        owned_count, rank_width, slab_width
    )
    theta_up = up_maps.astype(jnp.float32) - rate_up * up_gradient.reshape(
        owned_count, rank_width, out_width
    )
    denominator = SNAPS + 1.0
    new_mean_down = (SNAPS * mean_down + theta_down) / denominator
    new_square_down = (SNAPS * square_down + theta_down * theta_down) / denominator
    new_mean_up = (SNAPS * mean_up + theta_up) / denominator
    new_square_up = (SNAPS * square_up + theta_up * theta_up) / denominator
    return (projected, new_mean_down, new_square_down, new_mean_up, new_square_up)


def solution(mesh):
    placed = (
        P("dp", "fsdp"),
        P("dp", "fsdp"),
        P("fsdp", "dp"),
        P("dp", None, "fsdp"),
        P("dp", None, "fsdp"),
        P("dp", None, "fsdp"),
        P("dp", None, "fsdp"),
        P("dp", None, "fsdp"),
        P("dp", None, "fsdp"),
        P("dp"),
        P(),
    )
    return jax.shard_map(
        body,
        mesh=mesh,
        in_specs=placed,
        out_specs=(
            P("dp", "fsdp"),
            P("dp", None, "fsdp"),
            P("dp", None, "fsdp"),
            P("dp", None, "fsdp"),
            P("dp", None, "fsdp"),
        ),
        check_vma=False,
    )
```

profile of v0, /device:TPU:1, one launch (start us, length us, event | category | flops | bytes accessed | tf_op | source)
XLA Modules:
  0.0 313.1 jit_solution(14908360612011092690)
XLA Ops:
  7.2 0.0 copy-start.4
  7.2 0.0 all-gather.2.cloned.1.call-start
  7.2 0.7 all-gather.2.cloned.1.call-update
  7.9 0.0 copy-start
  7.9 1.1 reshape.130
  9.0 0.8 select_reduce_fusion
  9.8 0.2 convert_reduce_fusion
  10.1 0.2 convolution_convert_fusion.2
  10.3 0.0 copy-start.1
  10.3 0.9 reshape.131
  11.2 16.8 %all-to-all-start.3 = ((bf16[32,24,256]{2,1,0:T(8,128)(2,1)}), bf16[32,24,256]{2,1,0:T(8,128)(2,1)S(1)}, u32[]{:S(2)}, u32[]{:S(2)}) async-start(bf16[32,24,256]{2,1,0:T(8,128)(2,1)} %reshape.131), calls=%async_computation.3 | async-start | bytes 786432 | tf_op jit(solution)/shard_map/all_to_all | solution.py:77
  28.0 1.2 reshape.122
  29.2 0.3 convolution_convert_fusion.1
  29.5 1.2 reshape.123
  30.8 27.3 %all-to-all-done.3 = bf16[32,24,256]{2,1,0:T(8,128)(2,1)S(1)} async-done(((bf16[32,24,256]{2,1,0:T(8,128)(2,1)}), bf16[32,24,256]{2,1,0:T(8,128)(2,1)S(1)}, u32[]{:S(2)}, u32[]{:S(2)}) %all-to-all-start.3) | async-done | bytes 393248 | tf_op jit(solution)/shard_map/all_to_all | solution.py:77
  58.1 4.6 %all-to-all-start.1 = ((bf16[32,24,512]{2,1,0:T(8,128)(2,1)}), bf16[32,24,512]{2,1,0:T(8,128)(2,1)S(1)}, u32[]{:S(2)}, u32[]{:S(2)}) async-start(bf16[32,24,512]{2,1,0:T(8,128)(2,1)} %reshape.123), calls=%async_computation.1 | async-start | bytes 1572864 | tf_op jit(solution)/shard_map/all_to_all | solution.py:70
  62.7 0.0 all-reduce.3.cloned.1.call-start
  62.8 0.0 copy-done.4
  62.8 0.9 convolution_convert_fusion.3
  63.7 49.0 %all-to-all-done.1 = bf16[32,24,512]{2,1,0:T(8,128)(2,1)S(1)} async-done(((bf16[32,24,512]{2,1,0:T(8,128)(2,1)}), bf16[32,24,512]{2,1,0:T(8,128)(2,1)S(1)}, u32[]{:S(2)}, u32[]{:S(2)}) %all-to-all-start.1) | async-done | bytes 786464 | tf_op jit(solution)/shard_map/all_to_all | solution.py:70
  112.7 0.0 copy-done
  112.7 1.0 convolution_convert_fusion.4
  113.8 16.8 %all-gather.2.cloned.1.call-done = bf16[512,4096]{1,0:T(8,128)(2,1)} async-done(((bf16[512,128]{1,0:T(8,128)(2,1)}), bf16[512,4096]{1,0:T(8,128)(2,1)}) %all-gather.2.cloned.1.call-update) | async-done | bytes 4194320 | tf_op jit(solution)/shard_map/all_gather | solution.py:94
  130.6 0.0 copy-done.1
  130.6 5.7 %convolution_convert_fusion = bf16[384,4096]{1,0:T(8,128)(2,1)} fusion(bf16[384,512]{1,0:T(8,128)(2,1)S(1)} %copy-done.1, bf16[512,4096]{1,0:T(8,128)(2,1)} %all-gather.2.cloned.1.call-done), kind=kOutput, calls=%fused_computation | convolution fusion | flops 1612185600 | bytes 7733248 | tf_op jit(solution)/shard_map/dot_general | solution.py:92
  136.3 0.0 copy-start.5
  136.3 0.0 copy-start.6
  136.3 0.0 copy-start.2
  136.3 0.0 copy-start.3
  136.3 0.0 all-reduce.3.cloned.1.call-update
  136.4 0.1 fusion.1
  136.5 0.1 broadcast_in_dim.22
  136.6 0.1 copy.20
  136.7 0.7 copy.21
  137.4 7.0 %all-to-all-start = ((bf16[32,1,24]{2,1,0:T(2,128)(2,1)}), bf16[32,1,24]{2,1,0:T(2,128)(2,1)S(1)}, u32[]{:S(2)}, u32[]{:S(2)}) async-start(bf16[32,1,24]{2,1,0:T(2,128)(2,1)} %copy.21), calls=%async_computation | async-start | bytes 32768 | tf_op jit(solution)/shard_map/all_to_all | solution.py:84
  144.5 11.7 %all-to-all-done = bf16[32,1,24]{2,1,0:T(2,128)(2,1)S(1)} async-done(((bf16[32,1,24]{2,1,0:T(2,128)(2,1)}), bf16[32,1,24]{2,1,0:T(2,128)(2,1)S(1)}, u32[]{:S(2)}, u32[]{:S(2)}) %all-to-all-start) | async-done | bytes 1568 | tf_op jit(solution)/shard_map/all_to_all | solution.py:84
  156.2 0.1 convert_reduce_fusion.1
  156.3 0.1 reshape.133
  156.4 104.4 %all-reduce.3.cloned.1.call-done = (bf16[768,128]{1,0:T(8,128)(2,1)}, bf16[384,4096]{1,0:T(8,128)(2,1)}, bf16[768,128]{1,0:T(8,128)(2,1)}) async-done(((bf16[768,128]{1,0:T(8,128)(2,1)}, bf16[384,4096]{1,0:T(8,128)(2,1)}, bf16[768,128]{1,0:T(8,128)(2,1)}), (bf16[768,128]{1,0:T(8,128)(2,1)}, bf16[384,4096]{1,0:T(8,128)(2,1)}, bf16[768,128]{1,0:T(8,128)(2,1)})) %all-reduce.3.cloned.1.call-update) | async-done | bytes 3538960 | tf_op jit(solution)/shard_map/psum | solution.py:114
  260.8 2.0 fusion
  262.8 13.4 %all-to-all-start.2 = ((bf16[32,24,256]{2,1,0:T(8,128)(2,1)}), bf16[32,24,256]{2,1,0:T(8,128)(2,1)S(1)}, u32[]{:S(2)}, u32[]{:S(2)}) async-start(bf16[32,24,256]{2,1,0:T(8,128)(2,1)} %bitcast.6), calls=%async_computation.2 | async-start | bytes 786432 | tf_op jit(solution)/shard_map/all_to_all | solution.py:123
  276.2 1.3 convolution_multiply_fusion.2
  277.5 0.0 copy-done.5
  277.5 0.0 copy-done.6
  277.5 0.7 add_multiply_fusion.2
  278.2 1.4 convolution_multiply_fusion.1
  279.6 0.0 copy-done.2
  279.6 0.0 copy-done.3
  279.6 0.9 add_multiply_fusion
  280.5 23.6 %all-to-all-done.2 = bf16[32,24,256]{2,1,0:T(8,128)(2,1)S(1)} async-done(((bf16[32,24,256]{2,1,0:T(8,128)(2,1)}), bf16[32,24,256]{2,1,0:T(8,128)(2,1)S(1)}, u32[]{:S(2)}, u32[]{:S(2)}) %all-to-all-start.2) | async-done | bytes 393248 | tf_op jit(solution)/shard_map/all_to_all | solution.py:123
  304.1 0.2 reshape.128
  304.3 0.2 fusion.10
  304.6 0.1 reshape.129
  304.6 1.7 add_convert_fusion
  (4 shorter events, 0.0 us)
Async XLA Ops:
  7.2 55.6 %copy-start.4 = (bf16[2,64,256]{2,1,0:T(8,128)(2,1)S(1)}, bf16[2,64,256]{2,1,0:T(8,128)(2,1)}, u32[]{:S(2)}) copy-start(bf16[2,64,256]{2,1,0:T(8,128)(2,1)} %param.15) | copy-start | bytes 196612
  7.2 123.4 %all-gather.2.cloned.1.call-start = ((), (), s32[]{:S(2)}) async-start(), calls=%async_computation.4 | async-start | bytes 4325376 | tf_op jit(solution)/shard_map/all_gather | solution.py:94
  7.9 104.8 %copy-start = (bf16[2,64,512]{2,1,0:T(8,128)(2,1)S(1)}, bf16[2,64,512]{2,1,0:T(8,128)(2,1)}, u32[]{:S(2)}) copy-start(bf16[2,64,512]{2,1,0:T(8,128)(2,1)} %param.14) | copy-start | bytes 393220
  10.3 120.3 %copy-start.1 = (bf16[384,512]{1,0:T(8,128)(2,1)S(1)}, bf16[384,512]{1,0:T(8,128)(2,1)}, u32[]{:S(2)}) copy-start(bf16[384,512]{1,0:T(8,128)(2,1)} %param.11) | copy-start | bytes 1179652
  11.2 46.9 %all-to-all-start.3 = ((bf16[32,24,256]{2,1,0:T(8,128)(2,1)}), bf16[32,24,256]{2,1,0:T(8,128)(2,1)S(1)}, u32[]{:S(2)}, u32[]{:S(2)}) async-start(bf16[32,24,256]{2,1,0:T(8,128)(2,1)} %reshape.131), calls=%async_computation.3 | async-start | bytes 786432 | tf_op jit(solution)/shard_map/all_to_all | solution.py:77
  58.1 54.6 %all-to-all-start.1 = ((bf16[32,24,512]{2,1,0:T(8,128)(2,1)}), bf16[32,24,512]{2,1,0:T(8,128)(2,1)S(1)}, u32[]{:S(2)}, u32[]{:S(2)}) async-start(bf16[32,24,512]{2,1,0:T(8,128)(2,1)} %reshape.123), calls=%async_computation.1 | async-start | bytes 1572864 | tf_op jit(solution)/shard_map/all_to_all | solution.py:70
  62.7 198.1 %all-reduce.3.cloned.1.call-start = ((), (), s32[]{:S(2)}) async-start(), calls=%async_computation.5 | async-start | bytes 7077888 | tf_op jit(solution)/shard_map/psum | solution.py:114
  136.3 141.1 %copy-start.5 = (f32[2,64,256]{2,1,0:T(8,128)S(1)}, f32[2,64,256]{2,1,0:T(8,128)}, u32[]{:S(2)}) copy-start(f32[2,64,256]{2,1,0:T(8,128)} %param.19) | copy-start | bytes 393220
  136.3 141.1 %copy-start.6 = (f32[2,64,256]{2,1,0:T(8,128)S(1)}, f32[2,64,256]{2,1,0:T(8,128)}, u32[]{:S(2)}) copy-start(f32[2,64,256]{2,1,0:T(8,128)} %param.18) | copy-start | bytes 393220
  136.3 143.3 %copy-start.2 = (f32[2,64,512]{2,1,0:T(8,128)S(1)}, f32[2,64,512]{2,1,0:T(8,128)}, u32[]{:S(2)}) copy-start(f32[2,64,512]{2,1,0:T(8,128)} %param.17) | copy-start | bytes 786436
  136.3 143.3 %copy-start.3 = (f32[2,64,512]{2,1,0:T(8,128)S(1)}, f32[2,64,512]{2,1,0:T(8,128)}, u32[]{:S(2)}) copy-start(f32[2,64,512]{2,1,0:T(8,128)} %param.16) | copy-start | bytes 786436
  137.4 18.8 %all-to-all-start = ((bf16[32,1,24]{2,1,0:T(2,128)(2,1)}), bf16[32,1,24]{2,1,0:T(2,128)(2,1)S(1)}, u32[]{:S(2)}, u32[]{:S(2)}) async-start(bf16[32,1,24]{2,1,0:T(2,128)(2,1)} %copy.21), calls=%async_computation | async-start | bytes 32768 | tf_op jit(solution)/shard_map/all_to_all | solution.py:84
  262.8 41.4 %all-to-all-start.2 = ((bf16[32,24,256]{2,1,0:T(8,128)(2,1)}), bf16[32,24,256]{2,1,0:T(8,128)(2,1)S(1)}, u32[]{:S(2)}, u32[]{:S(2)}) async-start(bf16[32,24,256]{2,1,0:T(8,128)(2,1)} %bitcast.6), calls=%async_computation.2 | async-start | bytes 786432 | tf_op jit(solution)/shard_map/all_to_all | solution.py:123
Sparse Core Ops, SparseCore 0:
  10.1 120.4 all-gather.1
  136.5 124.2 all-reduce.2
where the time goes:
time: 314 us; the launch traced here: 313 us
  waiting for transfers between devices  234 us (75%)
  starting transfers between devices  41.9 us (13%)
  between operations  14.2 us (5%)
  matrix products  13.3 us (4%)
  local copies, waits for them, and re-layouts  5.7 us (2%)
  other arithmetic  4.4 us (1%)
    psum x1, waiting for transfers between devices, body(): lax.psum(down_part.astype(jnp.bfloat16), 'fsdp').astype(jnp.float32)  104 us
    all_to_all x1, waiting for transfers between devices, body(): lax.all_to_all(sent_inputs.reshape(dp_count, capacity * block_rows, slab_...  49 us
    all_to_all x1, waiting for transfers between devices, body(): lax.all_to_all(sent_grads.reshape(dp_count, capacity * block_rows, out_wi...  27.3 us
    all_to_all x1, waiting for transfers between devices, body(): lax.all_to_all(adapted_output.reshape(dp_count, capacity * block_rows, ou...  23.6 us
    all_gather x1, waiting for transfers between devices, body(): lax.all_gather(base_weight, 'dp', axis=1, tiled=True)  16.8 us
    all_to_all x1, starting transfers between devices, body(): lax.all_to_all(sent_grads.reshape(dp_count, capacity * block_rows, out_wi...  16.8 us
    all_to_all x1, starting transfers between devices, body(): lax.all_to_all(adapted_output.reshape(dp_count, capacity * block_rows, ou...  13.4 us
    all_to_all x1, waiting for transfers between devices, body(): lax.all_to_all(row_tags.reshape(dp_count, capacity * block_rows), 'dp', s...  11.7 us
  transfers between devices with their start and end apart: 6, of which 6 were waited for; matrix products, arithmetic and copies ran while one was open for 4% of the time, Pallas kernels for 0%

commit v1 on v0

v1 whole, which is shorter than its diff:
```python
import functools

import jax
import jax.numpy as jnp
from jax import lax
from jax.experimental import pallas as pl
from jax.experimental.pallas import tpu as pltpu
from jax.sharding import PartitionSpec as P

SNAPS = 2
BLK = 8

adapter_scale = 2.0
rate_down = 0.002
rate_up = 0.02
contract_last = (((1,), (1,)), ((), ()))
contract_first = (((0,), (0,)), ((), ()))
MESH = pl.DeviceIdType.MESH
GROUP = 4

f32 = jnp.float32
bf16 = jnp.bfloat16


def iota(shape, dim):
    return lax.broadcasted_iota(jnp.int32, shape, dim)


def to_column(row):
    n = row.shape[1]
    return jnp.sum(jnp.where(iota((n, n), 0) == iota((n, n), 1), row, 0), axis=1, keepdims=True)


def kernel(
    sizes,
    x_ref, g_ref, w_ref, d_ref, u_ref, member_ref, slot_ref,
    out_ref, gd_ref, gu_ref,
    w_all, disp_send, disp_recv, tag_send, tag_recv,
    part_send, part_recv, lr_send, lr_recv, lr_all, ret_send, ret_recv, acc,
    ring_r_send, ring_r_recv, ring_l_send, ring_l_recv, sib_send, sib_recv,
    disp_ssem, disp_rsem, tag_ssem, tag_rsem, part_ssem, part_rsem,
    rs_ssem, rs_rsem, ag_ssem, ag_rsem, ret_ssem, ret_rsem,
):
    n_dp, n_f, cap = sizes
    n_z = n_dp // 2
    half_z = n_z // 2
    rows, slab = x_ref.shape
    width = g_ref.shape[1]
    hs, hw = slab // 2, width // 2
    blocks = member_ref.shape[1]
    members = slot_ref.shape[1]
    chunk = cap * BLK
    me = lax.axis_index("dp")
    fs = lax.axis_index("fsdp")
    z, core = me // 2, me % 2
    right = lax.rem(z + 1, n_z) * 2 + core
    left = lax.rem(z + n_z - 1, n_z) * 2 + core
    sibling = z * 2 + (1 - core)

    def dp_copy(src, dst, send_sem, recv_sem, to):
        return pltpu.make_async_remote_copy(
            src_ref=src, dst_ref=dst, send_sem=send_sem, recv_sem=recv_sem,
            device_id=(to, fs), device_id_type=MESH,
        )

    def f_copy(src, dst, send_sem, recv_sem, to):
        return pltpu.make_async_remote_copy(
            src_ref=src, dst_ref=dst, send_sem=send_sem, recv_sem=recv_sem,
            device_id=(me, to), device_id_type=MESH,
        )

    barrier = pltpu.get_barrier_semaphore()

    @pl.loop(1, n_dp)
    def _(k):
        pl.semaphore_signal(barrier, inc=1, device_id=(lax.rem(me + k, n_dp), fs), device_id_type=MESH)

    @pl.loop(1, n_f)
    def _(k):
        pl.semaphore_signal(barrier, inc=1, device_id=(me, lax.rem(fs + k, n_f)), device_id_type=MESH)

    slot_col = to_column(slot_ref[...])
    slots = jnp.sum(
        jnp.where(iota((members, blocks), 0) == member_ref[...], slot_col, 0), axis=0, keepdims=True
    )
    owner = slots // 2
    local = slots - owner * 2
    owner_col = to_column(owner)
    earlier = (owner_col == owner) & (iota((blocks, blocks), 0) < iota((blocks, blocks), 1))
    position = jnp.sum(jnp.where(earlier, 1, 0), axis=0, keepdims=True)
    target = owner * cap + position
    target_col = to_column(target)
    local_col = to_column(local)
    row_target = (
        jnp.sum(
            jnp.where(iota((blocks, rows), 0) == iota((blocks, rows), 1) // BLK, target_col, 0),
            axis=0, keepdims=True,
        ) * BLK
        + iota((1, rows), 1) % BLK
    )
    row_target_col = (
        jnp.sum(
            jnp.where(iota((rows, blocks), 1) == iota((rows, blocks), 0) // BLK, target, 0),
            axis=1, keepdims=True,
        ) * BLK
        + iota((rows, 1), 0) % BLK
    )
    tag_send[0] = jnp.sum(
        jnp.where(target_col == iota((blocks, 128), 1), local_col, 0), axis=0, keepdims=True
    )
    tag_recv[pl.ds(me, 1)] = tag_send[...]
    w_all[pl.ds(z, 1), pl.ds(core, 1)] = w_ref[...].reshape(1, 1, *w_ref.shape)

    halves = [
        jnp.concatenate([x_ref[:, h * hs:(h + 1) * hs], g_ref[:, h * hw:(h + 1) * hw]], axis=1)
        for h in range(2)
    ]

    @pl.loop(0, n_dp // GROUP)
    def _(i):
        pick = jnp.where(
            iota((GROUP * chunk, rows), 0) + i * (GROUP * chunk) == row_target, 1.0, 0.0
        ).astype(bf16)
        both = [
            jnp.dot(pick, half, preferred_element_type=f32).reshape(GROUP, chunk, hs + hw)
            for half in halves
        ]
        disp_send[pl.ds(i * GROUP, GROUP)] = jnp.concatenate(both, axis=1).astype(bf16)

    disp_recv[pl.ds(me, 1)] = disp_send[pl.ds(me, 1)]

    pl.semaphore_wait(barrier, n_dp + n_f - 2)

    def ring_right(src_z, step):
        block = w_all.at[src_z, core]
        return dp_copy(block, block, ring_r_send.at[step], ring_r_recv.at[step], right)

    def ring_left(src_z, step):
        block = w_all.at[src_z, core]
        return dp_copy(block, block, ring_l_send.at[step], ring_l_recv.at[step], left)

    def to_sibling(src_z):
        block = w_all.at[src_z, core]
        return dp_copy(block, block, sib_send.at[src_z], sib_recv.at[src_z], sibling)

    def from_sibling(src_z):
        block = w_all.at[src_z, 1 - core]
        return dp_copy(block, block, sib_send.at[src_z], sib_recv.at[src_z], sibling)

    def start_ring():
        ring_right(z, 1).start()
        ring_left(z, 1).start()
        to_sibling(z).start()

    def disp_to(k):
        to = lax.rem(me + k, n_dp)
        return dp_copy(disp_send.at[to], disp_recv.at[me], disp_ssem.at[to], disp_rsem.at[me], to)

    def disp_from(p):
        return dp_copy(disp_send.at[p], disp_recv.at[p], disp_ssem.at[p], disp_rsem.at[p], p)

    def tag_to(k):
        to = lax.rem(me + k, n_dp)
        return dp_copy(tag_send.at[0], tag_recv.at[me], tag_ssem.at[to], tag_rsem.at[me], to)

    def tag_from(p):
        return dp_copy(tag_send.at[0], tag_recv.at[p], tag_ssem.at[p], tag_rsem.at[p], p)

    start_ring()

    @pl.loop(1, n_dp)
    def _(k):
        tag_to(k).start()
        disp_to(k).start()

    def part_to(j):
        return f_copy(part_send.at[j], part_recv.at[fs], part_ssem.at[j], part_rsem.at[fs], j)

    def part_from(j):
        return f_copy(part_send.at[j], part_recv.at[j], part_ssem.at[j], part_rsem.at[j], j)

    def term(j):
        from_sibling(j).wait_recv()
        part_send[pl.ds(j, 1)] = jnp.concatenate(
            [jnp.dot(x_ref[...], w_all[j, c], preferred_element_type=f32) for c in range(2)], axis=1
        ).astype(bf16)[None]

        @pl.when(j == fs)
        def _():
            part_recv[pl.ds(j, 1)] = part_send[pl.ds(j, 1)]

        @pl.when(j != fs)
        def _():
            part_to(j).start()

    def from_left(step):
        return lax.rem(z + n_z - step, n_z)

    def from_right(step):
        return lax.rem(z + step, n_z)

    term(z)

    @pl.loop(1, half_z)
    def _(s):
        ring_right(from_left(s), s).wait_recv()
        ring_right(from_left(s), s + 1).start()
        to_sibling(from_left(s)).start()
        ring_left(from_right(s), s).wait_recv()

        @pl.when(s < half_z - 1)
        def _():
            ring_left(from_right(s), s + 1).start()
        to_sibling(from_right(s)).start()

        @pl.when(s > 1)
        def _():
            @pl.loop(0, 2)
            def _(k):
                term(lax.rem(z + n_z + (s - 1) * (2 * k - 1), n_z))

    ring_right(from_left(half_z), half_z).wait_recv()
    to_sibling(from_left(half_z)).start()

    @pl.loop(0, 3)
    def _(k):
        term(lax.rem(z + n_z + jnp.where(k == 0, 1 - half_z, half_z - 2 + k), n_z))

    @pl.loop(1, n_dp)
    def _(k):
        p = lax.rem(me + n_dp - k, n_dp)
        tag_from(p).wait_recv()
        disp_from(p).wait_recv()

    first = iota((GROUP * chunk, 128), 1) < 64

    def tags_of(i):
        tags = tag_recv[pl.ds(i * GROUP, GROUP)]
        shape = (GROUP, chunk, 128)
        mine = iota(shape, 2) == me * cap + iota(shape, 1) // BLK
        tag = jnp.sum(jnp.where(mine, tags.astype(f32), 0.0), axis=2, keepdims=True)
        return jnp.broadcast_to(tag, shape).reshape(GROUP * chunk, 128) > 0.5

    def fold(value):
        value = value.reshape(GROUP, 2 * chunk, value.shape[1])
        return value[:, :chunk], value[:, chunk:]

    def projected(got, maps, half):
        one = lax.dot_general(got, maps[:, :half], contract_last, preferred_element_type=f32)
        two = lax.dot_general(got, maps[:, half:], contract_last, preferred_element_type=f32)
        return (fold(one)[0] + fold(two)[1]).reshape(GROUP * chunk, 128)

    @pl.loop(0, n_dp // GROUP)
    def _(i):
        got = disp_recv[pl.ds(i * GROUP, GROUP)].reshape(GROUP * 2 * chunk, hs + hw)
        low = projected(got[:, :hs], d_ref[...], hs)
        back = projected(got[:, hs:], u_ref[...], hw)
        tag = tags_of(i)
        low = jnp.where(tag, pltpu.roll(low, 64, 1), low)
        back = jnp.where(tag, back, pltpu.roll(back, 64, 1))
        lr_send[pl.ds(i * 2, 2)] = jnp.where(first, low, back).reshape(2, 2 * chunk, 128).astype(bf16)

    lr_recv[pl.ds(fs, 1)] = lr_send[pl.ds(fs, 1)]

    def rs_to(j):
        return f_copy(lr_send.at[j], lr_recv.at[fs], rs_ssem.at[j], rs_rsem.at[fs], j)

    def rs_from(j):
        return f_copy(lr_send.at[j], lr_recv.at[j], rs_ssem.at[j], rs_rsem.at[j], j)

    def ag_to(j):
        return f_copy(lr_all.at[fs], lr_all.at[fs], ag_ssem.at[j], ag_rsem.at[fs], j)

    def ag_from(j):
        return f_copy(lr_all.at[j], lr_all.at[j], ag_ssem.at[j], ag_rsem.at[j], j)

    def others(n, mine, act):
        @pl.loop(1, n)
        def _(k):
            act(lax.rem(mine + k, n))

    others(n_f, fs, lambda j: rs_to(j).start())
    others(n_f, fs, lambda j: rs_from(j).wait_recv())
    lr_all[pl.ds(fs, 1)] = jnp.sum(lr_recv[...].astype(f32), axis=0).astype(bf16)[None]
    others(n_f, fs, lambda j: ag_to(j).start())
    others(n_f, fs, lambda j: ag_from(j).wait_recv())

    def spread(i):
        value = lr_all[pl.ds(i * 2, 2)].reshape(GROUP * chunk, 128).astype(f32)
        turned = pltpu.roll(value, 64, 1)
        tag = tags_of(i)
        low = jnp.where(first, jnp.where(tag, 0.0, value), jnp.where(tag, turned, 0.0))
        back = jnp.where(first, jnp.where(tag, 0.0, turned), jnp.where(tag, value, 0.0))
        return low, back

    @pl.loop(0, n_dp // GROUP)
    def _(i):
        low, _ = spread(i)
        adapted = adapter_scale * jnp.dot(low.astype(bf16), u_ref[...], preferred_element_type=f32)
        adapted = adapted.reshape(GROUP, chunk, width)
        ret_send[pl.ds(i * GROUP, GROUP)] = jnp.concatenate(
            [adapted[:, :, :hw], adapted[:, :, hw:]], axis=1
        ).astype(bf16)

    def ret_to(p):
        return dp_copy(ret_send.at[p], ret_recv.at[me], ret_ssem.at[p], ret_rsem.at[me], p)

    def ret_from(p):
        return dp_copy(ret_send.at[p], ret_recv.at[p], ret_ssem.at[p], ret_rsem.at[p], p)

    others(n_dp, me, lambda p: ret_to(p).start())
    ret_recv[pl.ds(me, 1)] = ret_send[pl.ds(me, 1)]

    gd_ref[...] = jnp.zeros_like(gd_ref)
    gu_ref[...] = jnp.zeros_like(gu_ref)

    @pl.loop(0, n_dp // GROUP)
    def _(i):
        got = disp_recv[pl.ds(i * GROUP, GROUP)].reshape(GROUP * 2 * chunk, hs + hw)
        low, back = spread(i)
        low = low.reshape(GROUP, chunk, 128)
        back = back.reshape(GROUP, chunk, 128)
        zero = jnp.zeros_like(low)

        def part(value, h, rows_of):
            pair = [value, zero] if h == 0 else [zero, value]
            wide = jnp.concatenate(pair, axis=1).reshape(GROUP * 2 * chunk, 128).astype(bf16)
            return lax.dot_general(wide, rows_of, contract_first, preferred_element_type=f32)

        for h in range(2):
            gd_ref[:, h * hs:(h + 1) * hs] += part(back, h, got[:, :hs])
            gu_ref[:, h * hw:(h + 1) * hw] += part(low, h, got[:, hs:])

    others(n_f, fs, lambda j: part_from(j).wait_recv())
    acc[...] = part_recv[0].astype(f32)

    @pl.loop(1, n_f)
    def _(j):
        acc[...] += part_recv[j].astype(f32)

    others(n_dp, me, lambda p: ret_from(p).wait_recv())

    @pl.loop(0, n_dp // GROUP)
    def _(i):
        one, two = fold(
            ret_recv[pl.ds(i * GROUP, GROUP)].astype(f32).reshape(GROUP * 2 * chunk, hw)
        )
        value = jnp.concatenate([one, two], axis=2).reshape(GROUP * chunk, width).astype(bf16)
        pick = jnp.where(
            iota((rows, GROUP * chunk), 1) + i * (GROUP * chunk) == row_target_col, 1.0, 0.0
        ).astype(bf16)
        acc[...] += jnp.dot(pick, value, preferred_element_type=f32)

    out_ref[...] = acc[...].astype(bf16)

    ring_right(z, 1).wait_send()
    ring_left(z, 1).wait_send()
    to_sibling(z).wait_send()

    @pl.loop(1, half_z)
    def _(s):
        ring_right(from_left(s), s + 1).wait_send()
        to_sibling(from_left(s)).wait_send()

        @pl.when(s < half_z - 1)
        def _():
            ring_left(from_right(s), s + 1).wait_send()
        to_sibling(from_right(s)).wait_send()

    to_sibling(from_left(half_z)).wait_send()

    @pl.loop(1, n_dp)
    def _(k):
        tag_to(k).wait_send()
        disp_to(k).wait_send()
        ret_to(lax.rem(me + k, n_dp)).wait_send()

    @pl.loop(1, n_f)
    def _(k):
        j = lax.rem(fs + k, n_f)
        part_to(j).wait_send()
        rs_to(j).wait_send()
        ag_to(j).wait_send()


def fused(x, g, w, down, up, block_member, member_slot):
    n_dp, n_f = lax.axis_size("dp"), lax.axis_size("fsdp")
    rows, slab = x.shape
    width = g.shape[1]
    cap = 2 * block_member.shape[1] // n_dp
    chunk = cap * BLK
    n_z = n_dp // 2
    vmem = pl.BlockSpec(memory_space=pltpu.VMEM)
    dma = pltpu.SemaphoreType.DMA
    return pl.pallas_call(
        functools.partial(kernel, (n_dp, n_f, cap)),
        out_shape=(
            jax.ShapeDtypeStruct((rows, width), bf16),
            jax.ShapeDtypeStruct(down.shape, f32),
            jax.ShapeDtypeStruct(up.shape, f32),
        ),
        in_specs=[vmem] * 7,
        out_specs=(vmem,) * 3,
        scratch_shapes=[
            pltpu.VMEM((n_z, 2, *w.shape), bf16),
            pltpu.VMEM((n_dp, 2 * chunk, (slab + width) // 2), bf16),
            pltpu.VMEM((n_dp, 2 * chunk, (slab + width) // 2), bf16),
            pltpu.VMEM((1, 1, 128), jnp.int32),
            pltpu.VMEM((n_dp, 1, 128), jnp.int32),
            pltpu.VMEM((n_f, rows, width), bf16),
            pltpu.VMEM((n_f, rows, width), bf16),
            pltpu.VMEM((n_f, 2 * chunk, 128), bf16),
            pltpu.VMEM((n_f, 2 * chunk, 128), bf16),
            pltpu.VMEM((n_f, 2 * chunk, 128), bf16),
            pltpu.VMEM((n_dp, 2 * chunk, width // 2), bf16),
            pltpu.VMEM((n_dp, 2 * chunk, width // 2), bf16),
            pltpu.VMEM((rows, width), f32),
            dma((n_z // 2 + 1,)), dma((n_z // 2 + 1,)), dma((n_z // 2 + 1,)), dma((n_z // 2 + 1,)),
            dma((n_z,)), dma((n_z,)),
            dma((n_dp,)), dma((n_dp,)), dma((n_dp,)), dma((n_dp,)),
            dma((n_f,)), dma((n_f,)), dma((n_f,)), dma((n_f,)), dma((n_f,)), dma((n_f,)),
            dma((n_dp,)), dma((n_dp,)),
        ],
        compiler_params=pltpu.CompilerParams(
            collective_id=0, has_side_effects=True, vmem_limit_bytes=40 * 1024 * 1024
        ),
        name="adapter_step",
    )(x, g, w, down, up, block_member, member_slot)


def body(
    inputs, out_grad, base_weight, down_maps, up_maps,
    mean_down, square_down, mean_up, square_up, block_member, member_slot,
):
    owned, rank, slab_width = down_maps.shape
    out_width = up_maps.shape[2]
    projected, down_gradient, up_gradient = fused(
        inputs,
        out_grad,
        base_weight,
        down_maps.reshape(owned * rank, slab_width),
        up_maps.reshape(owned * rank, out_width),
        block_member.reshape(1, -1),
        member_slot.reshape(1, -1),
    )
    theta_down = down_maps.astype(f32) - (rate_down * adapter_scale) * down_gradient.reshape(down_maps.shape)
    theta_up = up_maps.astype(f32) - (rate_up * adapter_scale) * up_gradient.reshape(up_maps.shape)
    denominator = SNAPS + 1.0
    new_mean_down = (SNAPS * mean_down + theta_down) / denominator
    new_square_down = (SNAPS * square_down + theta_down * theta_down) / denominator
    new_mean_up = (SNAPS * mean_up + theta_up) / denominator
    new_square_up = (SNAPS * square_up + theta_up * theta_up) / denominator
    return (projected, new_mean_down, new_square_down, new_mean_up, new_square_up)


def solution(mesh):
    split = P("dp", None, "fsdp")
    placed = (P("dp", "fsdp"), P("dp", "fsdp"), P("fsdp", "dp")) + (split,) * 6 + (P("dp"), P())
    return jax.shard_map(
        body,
        mesh=mesh,
        in_specs=placed,
        out_specs=(P("dp", "fsdp"),) + (split,) * 4,
        check_vma=False,
    )
```

time: 314 us -> 187 us (0.60)
  waiting for transfers between devices: 234 us -> 0 us
  Pallas kernels: 0 us -> 176 us
  starting transfers between devices: 41.9 us -> 0 us
  between operations: 14.2 us -> 0.7 us
  matrix products: 13.3 us -> 0 us
    pallas_call x0 -> x1, Pallas kernels: none -> 176 us  [fused(): pl.pallas_call(functools.partial(kernel, (n_dp, n_f, cap)), out_shape=(ja...]
    all_to_all x4 -> x0, waiting for transfers between devices: 112 us -> none  [the longest x1 49 us: body(): lax.all_to_all(sent_inputs.reshape(dp_count, capacity * block_rows, slab_...]
    psum x1 -> x0, waiting for transfers between devices: 104 us -> none  [body(): lax.psum(down_part.astype(jnp.bfloat16), 'fsdp').astype(jnp.float32)]
    all_to_all x4 -> x0, starting transfers between devices: 41.8 us -> none  [the longest x1 16.8 us: body(): lax.all_to_all(sent_grads.reshape(dp_count, capacity * block_rows, out_wi...]
    all_gather x1 -> x0, waiting for transfers between devices: 16.8 us -> none  [body(): lax.all_gather(base_weight, 'dp', axis=1, tiled=True)]
    dot_general x10 -> x0, matrix products: 13.3 us -> none  [the longest x1 5.73 us: body(): jnp.dot(inputs, lax.all_gather(base_weight, 'dp', axis=1, tiled=True), pr...]
    unnamed x14 -> x23, local copies, waits for them, and re-layouts: 0.03 us -> 7.83 us
    reshape x6 -> x0, local copies, waits for them, and re-layouts: 4.65 us -> none  [the longest x1 1.25 us: body(): sent_inputs.reshape(dp_count, capacity * block_rows, slab_width)]
  transfers between devices with their start and end apart: 6 -> 0, of which waited for: 6 -> 0; matrix products, arithmetic and copies ran while one was open for 4% -> 0% of each run, Pallas kernels for 0% -> 0%
where the time goes in v1:
time: 187 us; the launch traced here: 186 us
  Pallas kernels  176 us (94%)
  local copies, waits for them, and re-layouts  7.83 us (4%)
    pallas_call x1, Pallas kernels, fused(): pl.pallas_call(functools.partial(kernel, (n_dp, n_f, cap)), out_shape=(ja...  176 us
    unnamed x23, local copies, waits for them, and re-layouts  7.83 us

profile of v1, /device:TPU:1, one launch (start us, length us, event | category | flops | bytes accessed | tf_op | source)
XLA Modules:
  0.0 186.1 jit_solution(11241236262188935306)
XLA Ops:
  0.6 0.0 copy-start.5
  0.6 0.0 copy-start.6
  0.7 0.6 copy-done.5
  1.3 0.0 copy-done.6
  1.3 0.0 copy-start
  1.3 0.9 copy-done
  2.2 0.0 copy-start.1
  2.2 1.0 copy-done.1
  3.2 0.0 copy-start.2
  3.2 0.8 copy-done.2
  4.0 0.0 copy-start.3
  4.0 0.9 copy-done.3
  5.0 0.0 copy-start.4
  5.0 0.9 copy-done.4
  5.9 175.9 %adapter_step.1 = (bf16[384,256]{1,0:T(8,128)(2,1)S(1)}, f32[128,512]{1,0:T(8,128)S(1)}, f32[128,256]{1,0:T(8,128)S(1)}) custom-call(bf16[384,512]{1,0:T(8,128)(2,1)S(1)} %copy-done.1, bf16[384,256]{1,0:T(8,128)(2,1)S(1)} %copy-done.3, bf16[512,128]{1,0:T(8,128)(2,1)S(1)} %copy-done.4, bf16[128,512]{1,0:T(8,128)(2,1)S(1)} %bitcast.6, ...), custom_call_target="tpu_custom_call" | custom-call | tf_op jit(solution)/shard_map/adapter_step/pallas_call | solution.py:395
  181.8 0.0 copy-start.7
  181.8 0.0 copy-start.8
  181.9 0.9 copy-done.7
  182.7 0.1 copy-done.8
  182.8 0.9 add_multiply_fusion
  183.7 0.0 copy-start.9
  183.7 0.0 copy-start.10
  183.7 0.9 copy-done.9
  184.6 0.1 copy-done.10
  184.7 0.7 add_multiply_fusion.2
  185.4 0.7 copy.17
  (2 shorter events, 0.0 us)
Async XLA Ops:
  0.6 0.7 copy-start.5
  0.6 0.7 copy-start.6
  1.3 0.9 copy-start
  2.2 1.0 copy-start.1
  3.2 0.8 copy-start.2
  4.0 0.9 copy-start.3
  5.0 0.9 copy-start.4
  181.8 1.0 copy-start.7
  181.8 1.0 copy-start.8
  183.7 0.9 copy-start.9
  183.7 1.0 copy-start.10

commit v2 on v1

v2 whole, which is shorter than its diff:
```python
import functools

import jax
import jax.numpy as jnp
from jax import lax
from jax.experimental import pallas as pl
from jax.experimental.pallas import tpu as pltpu
from jax.sharding import PartitionSpec as P

SNAPS = 2
BLK = 8

adapter_scale = 2.0
rate_down = 0.002
rate_up = 0.02
contract_last = (((1,), (1,)), ((), ()))
contract_first = (((0,), (0,)), ((), ()))
MESH = pl.DeviceIdType.MESH
GROUP = 4
PIECES = 3

f32 = jnp.float32
bf16 = jnp.bfloat16


def iota(shape, dim):
    return lax.broadcasted_iota(jnp.int32, shape, dim)


def to_column(row):
    n = row.shape[1]
    return jnp.sum(jnp.where(iota((n, n), 0) == iota((n, n), 1), row, 0), axis=1, keepdims=True)


def kernel(
    sizes,
    x_hbm, g_hbm, w_hbm, d_hbm, u_hbm, member_ref, slot_ref,
    out_ref, gd_ref, gu_ref,
    x_ref, g_ref, d_ref, u_ref, wt_all, disp_send, disp_recv,
    part_send, part_recv, lr_send, lr_recv, lr_all, ret_send, ret_recv, acc,
    in_sem, ring_r_send, ring_r_recv, ring_l_send, ring_l_recv, sib_send, sib_recv,
    disp_ssem, disp_rsem, part_ssem, part_rsem,
    rs_ssem, rs_rsem, ag_ssem, ag_rsem, ret_ssem, ret_rsem,
):
    n_dp, n_f, cap = sizes
    n_z = n_dp // 2
    half_z = n_z // 2
    rows, slab = x_hbm.shape
    width = g_hbm.shape[1]
    hs, hw = slab // 2, width // 2
    blocks = member_ref.shape[1]
    members = slot_ref.shape[1]
    chunk = cap * BLK
    depth = w_hbm.shape[0]
    me = lax.axis_index("dp")
    fs = lax.axis_index("fsdp")
    z, core = me // 2, me % 2
    right = lax.rem(z + 1, n_z) * 2 + core
    left = lax.rem(z + n_z - 1, n_z) * 2 + core
    sibling = z * 2 + (1 - core)
    last = n_dp - 2 + core

    def offset(m):
        return jnp.where(m % 2 == 1, half_z - (m + 1) // 2, m // 2 + n_z - half_z)

    def receiver(i):
        return lax.rem(z + offset(i // 2), n_z) * 2 + i % 2

    def sender(i):
        return lax.rem(z + n_z - lax.rem(offset(i // 2), n_z), n_z) * 2 + i % 2

    def places(start, stop, act):
        @pl.loop(start, stop)
        def _(i):
            @pl.when(i != last)
            def _():
                act(i)

    def dp_copy(src, dst, send_sem, recv_sem, to):
        return pltpu.make_async_remote_copy(
            src_ref=src, dst_ref=dst, send_sem=send_sem, recv_sem=recv_sem,
            device_id=(to, fs), device_id_type=MESH,
        )

    def f_copy(src, dst, send_sem, recv_sem, to):
        return pltpu.make_async_remote_copy(
            src_ref=src, dst_ref=dst, send_sem=send_sem, recv_sem=recv_sem,
            device_id=(me, to), device_id_type=MESH,
        )

    barrier = pltpu.get_barrier_semaphore()
    loads = [
        pltpu.make_async_copy(src, dst, in_sem.at[i])
        for i, (src, dst) in enumerate(
            [(x_hbm, x_ref), (g_hbm, g_ref), (w_hbm, wt_all.at[z, core, pl.ds(0, depth)]), (d_hbm, d_ref), (u_hbm, u_ref)]
        )
    ]
    for load in loads:
        load.start()

    @pl.loop(1, n_dp)
    def _(k):
        pl.semaphore_signal(barrier, inc=1, device_id=(lax.rem(me + k, n_dp), fs), device_id_type=MESH)

    @pl.loop(1, n_f)
    def _(k):
        pl.semaphore_signal(barrier, inc=1, device_id=(me, lax.rem(fs + k, n_f)), device_id_type=MESH)

    slot_col = to_column(slot_ref[...])
    slots = jnp.sum(
        jnp.where(iota((members, blocks), 0) == member_ref[...], slot_col, 0), axis=0, keepdims=True
    )
    owner = slots // 2
    local = slots - owner * 2
    owner_col = to_column(owner)
    earlier = (owner_col == owner) & (iota((blocks, blocks), 0) < iota((blocks, blocks), 1))
    position = jnp.sum(jnp.where(earlier, 1, 0), axis=0, keepdims=True)
    target = owner * cap + position
    target_col = to_column(target)
    local_col = to_column(local)
    row_target = (
        jnp.sum(
            jnp.where(iota((blocks, rows), 0) == iota((blocks, rows), 1) // BLK, target_col, 0),
            axis=0, keepdims=True,
        ) * BLK
        + iota((1, rows), 1) % BLK
    )
    row_target_col = (
        jnp.sum(
            jnp.where(iota((rows, blocks), 1) == iota((rows, blocks), 0) // BLK, target, 0),
            axis=1, keepdims=True,
        ) * BLK
        + iota((rows, 1), 0) % BLK
    )
    tags = jnp.sum(
        jnp.where(target_col == iota((blocks, 128), 1), local_col, 0), axis=0, keepdims=True
    )
    wt_all[pl.ds(z, 1), pl.ds(core, 1), pl.ds(depth, 16)] = jnp.broadcast_to(
        tags.astype(f32), (16, 128)
    ).astype(bf16)[None, None]
    for load in loads:
        load.wait()

    halves = [
        jnp.concatenate([x_ref[:, h * hs:(h + 1) * hs], g_ref[:, h * hw:(h + 1) * hw]], axis=1)
        for h in range(2)
    ]

    @pl.loop(0, n_dp // GROUP)
    def _(i):
        pick = jnp.where(
            iota((GROUP * chunk, rows), 0) + i * (GROUP * chunk) == row_target, 1.0, 0.0
        ).astype(bf16)
        both = [
            jnp.dot(pick, half, preferred_element_type=f32).reshape(GROUP, chunk, hs + hw)
            for half in halves
        ]
        disp_send[pl.ds(i * GROUP, GROUP)] = jnp.concatenate(both, axis=1).astype(bf16)

    disp_recv[pl.ds(last, 1)] = disp_send[pl.ds(me, 1)]

    pl.semaphore_wait(barrier, n_dp + n_f - 2)

    piece = wt_all.shape[2] // PIECES

    def ring_right(src_z, step, q):
        block = wt_all.at[src_z, core, pl.ds(pl.multiple_of(q * piece, piece), piece)]
        at = step * PIECES + q
        return dp_copy(block, block, ring_r_send, ring_r_recv.at[at], right)

    def ring_left(src_z, step, q):
        block = wt_all.at[src_z, core, pl.ds(pl.multiple_of(q * piece, piece), piece)]
        at = step * PIECES + q
        return dp_copy(block, block, ring_l_send, ring_l_recv.at[at], left)

    def to_sibling(src_z):
        block = wt_all.at[src_z, core]
        return dp_copy(block, block, sib_send, sib_recv.at[src_z], sibling)

    def from_sibling(src_z):
        block = wt_all.at[src_z, 1 - core]
        return dp_copy(block, block, sib_send, sib_recv.at[src_z], sibling)

    def start_ring():
        @pl.loop(0, PIECES)
        def _(q):
            ring_right(z, 1, q).start()
            ring_left(z, 1, q).start()

        to_sibling(z).start()

    half_places = n_dp // 2

    def disp_to(i):
        to, at = receiver(i), i // 2 * 2 + core
        return dp_copy(disp_send.at[to], disp_recv.at[at], disp_ssem, disp_rsem.at[i // half_places], to)

    def several(buffer, count, send_sem, recv_sem):
        blocks_of = buffer.at[pl.ds(0, count)]
        return dp_copy(blocks_of, blocks_of, send_sem, recv_sem, sibling)

    start_ring()

    def part_to(j):
        return f_copy(part_send.at[j], part_recv.at[fs], part_ssem, part_rsem, j)

    def term(j):
        from_sibling(j).wait_recv()
        part_send[pl.ds(j, 1)] = jnp.concatenate(
            [jnp.dot(x_ref[...], wt_all[j, c, pl.ds(0, depth)], preferred_element_type=f32) for c in range(2)],
            axis=1,
        ).astype(bf16)[None]

        @pl.when(j == fs)
        def _():
            part_recv[pl.ds(j, 1)] = part_send[pl.ds(j, 1)]

        @pl.when(j != fs)
        def _():
            part_to(j).start()

    def from_left(step):
        return lax.rem(z + n_z - step, n_z)

    def from_right(step):
        return lax.rem(z + step, n_z)

    term(z)

    @pl.loop(1, half_z)
    def _(s):
        @pl.loop(0, PIECES)
        def _(q):
            ring_right(from_left(s), s, q).wait_recv()
            ring_right(from_left(s), s + 1, q).start()
            ring_left(from_right(s), s, q).wait_recv()

            @pl.when(s < half_z - 1)
            def _():
                ring_left(from_right(s), s + 1, q).start()

            @pl.when((s > 1) & (q != 1))
            def _():
                term(lax.rem(z + n_z + (s - 1) * (q - 1), n_z))

        to_sibling(from_left(s)).start()
        to_sibling(from_right(s)).start()

    places(0, n_dp, lambda i: disp_to(i).start())

    @pl.loop(0, PIECES)
    def _(q):
        ring_right(from_left(half_z), half_z, q).wait_recv()

    to_sibling(from_left(half_z)).start()

    @pl.loop(0, 3)
    def _(k):
        term(lax.rem(z + n_z + jnp.where(k == 0, 1 - half_z, half_z - 2 + k), n_z))

    first = iota((GROUP * chunk, 128), 1) < 64

    def tags_of(sources, lanes):
        each = []
        for source, lane in zip(sources, lanes):
            row = wt_all[source // 2, source % 2, pl.ds(depth, 16)].astype(f32)[:1]
            mine = iota((chunk, 128), 1) == lane + iota((chunk, 128), 0) // BLK
            tag = jnp.sum(jnp.where(mine, row, 0.0), axis=1, keepdims=True)
            each.append(jnp.broadcast_to(tag, (chunk, 128)))
        return jnp.concatenate(each, axis=0) > 0.5

    def got_tags(i):
        return tags_of([sender(i * GROUP + k) for k in range(GROUP)], [me * cap] * GROUP)

    def fold(value):
        value = value.reshape(GROUP, 2 * chunk, value.shape[1])
        return value[:, :chunk], value[:, chunk:]

    def projected(got, maps, half):
        one = lax.dot_general(got, maps[:, :half], contract_last, preferred_element_type=f32)
        two = lax.dot_general(got, maps[:, half:], contract_last, preferred_element_type=f32)
        return (fold(one)[0] + fold(two)[1]).reshape(GROUP * chunk, 128)

    def project(i):
        got = disp_recv[pl.ds(i * GROUP, GROUP)].reshape(GROUP * 2 * chunk, hs + hw)
        low = projected(got[:, :hs], d_ref[...], hs)
        back = projected(got[:, hs:], u_ref[...], hw)
        tag = got_tags(i)
        low = jnp.where(tag, pltpu.roll(low, 64, 1), low)
        back = jnp.where(tag, back, pltpu.roll(back, 64, 1))
        lr_send[pl.ds(i * 2, 2)] = jnp.where(first, low, back).reshape(2, 2 * chunk, 128).astype(bf16)

    def rs_to(j):
        return f_copy(lr_send.at[j], lr_recv.at[fs], rs_ssem, rs_rsem, j)

    def ag_to(j):
        return f_copy(lr_all.at[fs], lr_all.at[fs], ag_ssem, ag_rsem.at[fs // (n_f // 2)], j)

    def others(n, mine, act):
        @pl.loop(1, n)
        def _(k):
            act(lax.rem(mine + k, n))

    def but_me(start, stop, act):
        @pl.loop(start, stop)
        def _(j):
            @pl.when(j != fs)
            def _():
                act(j)

    def by_slot(value, tag):
        turned = pltpu.roll(value, 64, 1)
        low = jnp.where(first, jnp.where(tag, 0.0, value), jnp.where(tag, turned, 0.0))
        back = jnp.where(first, jnp.where(tag, 0.0, turned), jnp.where(tag, value, 0.0))
        return low, back

    def ranked(i):
        return lr_all[pl.ds(i * 2, 2)].reshape(GROUP * chunk, 128).astype(f32)

    def ret_to(i):
        to, at = sender(i), i // 2 * 2 + core
        return dp_copy(ret_send.at[i], ret_recv.at[at], ret_ssem, ret_rsem.at[i // half_places], to)

    def adapt(i):
        low, _ = by_slot(ranked(i), got_tags(i))
        adapted = adapter_scale * jnp.dot(low.astype(bf16), u_ref[...], preferred_element_type=f32)
        adapted = adapted.reshape(GROUP, chunk, width)
        ret_send[pl.ds(i * GROUP, GROUP)] = jnp.concatenate(
            [adapted[:, :, :hw], adapted[:, :, hw:]], axis=1
        ).astype(bf16)

    def take(i):
        one, two = fold(ret_recv[pl.ds(i * GROUP, GROUP)].astype(f32).reshape(GROUP * 2 * chunk, hw))
        value = jnp.concatenate([one, two], axis=2).reshape(GROUP * chunk, width).astype(bf16)
        goal = iota((1, GROUP * chunk), 1) % chunk
        place = iota((1, GROUP * chunk), 1) // chunk
        for k in range(GROUP):
            goal = jnp.where(place == k, goal + receiver(i * GROUP + k) * chunk, goal)
        pick = jnp.where(goal == row_target_col, 1.0, 0.0).astype(bf16)
        acc[...] += jnp.dot(pick, value, preferred_element_type=f32)

    def count(half):
        return half_places - half

    def arrive(half):
        several(disp_recv, count(half), disp_ssem, disp_rsem.at[half]).wait_recv()

    groups = n_dp // GROUP // 2

    def scatter(half):
        low_j, high_j = half * (n_f // 2), (half + 1) * (n_f // 2)
        pl.loop(half * groups, (half + 1) * groups)(project)
        but_me(low_j, high_j, lambda j: rs_to(j).start())

    def reduce(half):
        @pl.when(fs // (n_f // 2) == half)
        def _():
            lr_recv[pl.ds(fs, 1)] = lr_send[pl.ds(fs, 1)]
            several(lr_recv, n_f - 1, rs_ssem, rs_rsem).wait_recv()
            lr_all[pl.ds(fs, 1)] = jnp.sum(lr_recv[...].astype(f32), axis=0).astype(bf16)[None]
            others(n_f, fs, lambda j: ag_to(j).start())

    def give_back(half):
        mine = fs // (n_f // 2) == half
        for is_mine, chunks in ((True, n_f // 2 - 1), (False, n_f // 2)):
            @pl.when(mine == is_mine)
            def _():
                several(lr_all, chunks, ag_ssem, ag_rsem.at[half]).wait_recv()

        pl.loop(half * groups, (half + 1) * groups)(adapt)
        places(half * half_places, (half + 1) * half_places, lambda i: ret_to(i).start())

    def gradients(i):
        got = disp_recv[pl.ds(i * GROUP, GROUP)].reshape(GROUP * 2 * chunk, hs + hw)
        low, back = by_slot(ranked(i), got_tags(i))
        low = low.reshape(GROUP, chunk, 128)
        back = back.reshape(GROUP, chunk, 128)
        zero = jnp.zeros_like(low)

        def part(value, h, rows_of):
            pair = [value, zero] if h == 0 else [zero, value]
            wide = jnp.concatenate(pair, axis=1).reshape(GROUP * 2 * chunk, 128).astype(bf16)
            return lax.dot_general(wide, rows_of, contract_first, preferred_element_type=f32)

        for h in range(2):
            gd_ref[:, h * hs:(h + 1) * hs] += part(back, h, got[:, :hs])
            gu_ref[:, h * hw:(h + 1) * hw] += part(low, h, got[:, hs:])

    def ret_arrive(half):
        several(ret_recv, count(half), ret_ssem, ret_rsem.at[half]).wait_recv()
        pl.loop(half * groups, (half + 1) * groups)(take)

    arrive(0)
    scatter(0)
    reduce(0)
    give_back(0)
    gd_ref[...] = jnp.zeros_like(gd_ref)
    gu_ref[...] = jnp.zeros_like(gu_ref)
    arrive(1)
    scatter(1)

    several(part_recv, n_f - 1, part_ssem, part_rsem).wait_recv()
    acc[...] = part_recv[0].astype(f32)

    @pl.loop(1, n_f)
    def _(j):
        acc[...] += part_recv[j].astype(f32)

    reduce(1)
    pl.loop(0, groups)(gradients)
    give_back(1)
    ret_recv[pl.ds(last, 1)] = ret_send[pl.ds(last, 1)]
    pl.loop(groups, 2 * groups)(gradients)
    ret_arrive(0)
    ret_arrive(1)
    out_ref[...] = acc[...].astype(bf16)

    dp_copy(
        wt_all.at[pl.ds(0, half_z), 0], wt_all.at[pl.ds(0, half_z), 0], ring_r_send, ring_r_recv.at[0], right
    ).wait_send()
    dp_copy(
        wt_all.at[pl.ds(0, half_z - 1), 0], wt_all.at[pl.ds(0, half_z - 1), 0], ring_l_send, ring_l_recv.at[0], left
    ).wait_send()
    dp_copy(wt_all.at[:, 0], wt_all.at[:, 0], sib_send, sib_recv.at[0], sibling).wait_send()
    several(disp_send, n_dp - 1, disp_ssem, disp_rsem.at[0]).wait_send()
    several(part_send, n_f - 1, part_ssem, part_rsem).wait_send()
    several(lr_send, n_f - 1, rs_ssem, rs_rsem).wait_send()
    several(lr_all, n_f - 1, ag_ssem, ag_rsem.at[0]).wait_send()
    several(ret_send, n_dp - 1, ret_ssem, ret_rsem.at[0]).wait_send()


def fused(x, g, w, down, up, block_member, member_slot):
    n_dp, n_f = lax.axis_size("dp"), lax.axis_size("fsdp")
    rows, slab = x.shape
    width = g.shape[1]
    cap = 2 * block_member.shape[1] // n_dp
    chunk = cap * BLK
    n_z = n_dp // 2
    vmem = pl.BlockSpec(memory_space=pltpu.VMEM)
    hbm = pl.BlockSpec(memory_space=pltpu.HBM)
    dma = pltpu.SemaphoreType.DMA
    hops = (n_z // 2 + 1) * PIECES
    return pl.pallas_call(
        functools.partial(kernel, (n_dp, n_f, cap)),
        out_shape=(
            jax.ShapeDtypeStruct((rows, width), bf16),
            jax.ShapeDtypeStruct(down.shape, f32),
            jax.ShapeDtypeStruct(up.shape, f32),
        ),
        in_specs=[hbm] * 5 + [vmem] * 2,
        out_specs=(vmem,) * 3,
        scratch_shapes=[
            pltpu.VMEM(x.shape, bf16), pltpu.VMEM(g.shape, bf16),
            pltpu.VMEM(down.shape, bf16), pltpu.VMEM(up.shape, bf16),
            pltpu.VMEM((n_z, 2, w.shape[0] + 16, 128), bf16),
            pltpu.VMEM((n_dp, 2 * chunk, (slab + width) // 2), bf16),
            pltpu.VMEM((n_dp, 2 * chunk, (slab + width) // 2), bf16),
            pltpu.VMEM((n_f, rows, width), bf16),
            pltpu.VMEM((n_f, rows, width), bf16),
            pltpu.VMEM((n_f, 2 * chunk, 128), bf16),
            pltpu.VMEM((n_f, 2 * chunk, 128), bf16),
            pltpu.VMEM((n_f, 2 * chunk, 128), bf16),
            pltpu.VMEM((n_dp, 2 * chunk, width // 2), bf16),
            pltpu.VMEM((n_dp, 2 * chunk, width // 2), bf16),
            pltpu.VMEM((rows, width), f32),
            dma((5,)), dma, dma((hops,)), dma, dma((hops,)), dma, dma((n_z,)),
            dma, dma((2,)), dma, dma, dma, dma, dma, dma((2,)), dma, dma((2,)),
        ],
        compiler_params=pltpu.CompilerParams(
            collective_id=0, has_side_effects=True, vmem_limit_bytes=40 * 1024 * 1024
        ),
        name="adapter_step",
    )(x, g, w, down, up, block_member, member_slot)


def body(
    inputs, out_grad, base_weight, down_maps, up_maps,
    mean_down, square_down, mean_up, square_up, block_member, member_slot,
):
    owned, rank, slab_width = down_maps.shape
    out_width = up_maps.shape[2]
    projected, down_gradient, up_gradient = fused(
        inputs,
        out_grad,
        base_weight,
        down_maps.reshape(owned * rank, slab_width),
        up_maps.reshape(owned * rank, out_width),
        block_member.reshape(1, -1),
        member_slot.reshape(1, -1),
    )
    theta_down = down_maps.astype(f32) - (rate_down * adapter_scale) * down_gradient.reshape(down_maps.shape)
    theta_up = up_maps.astype(f32) - (rate_up * adapter_scale) * up_gradient.reshape(up_maps.shape)
    denominator = SNAPS + 1.0
    new_mean_down = (SNAPS * mean_down + theta_down) / denominator
    new_square_down = (SNAPS * square_down + theta_down * theta_down) / denominator
    new_mean_up = (SNAPS * mean_up + theta_up) / denominator
    new_square_up = (SNAPS * square_up + theta_up * theta_up) / denominator
    return (projected, new_mean_down, new_square_down, new_mean_up, new_square_up)


def solution(mesh):
    split = P("dp", None, "fsdp")
    placed = (P("dp", "fsdp"), P("dp", "fsdp"), P("fsdp", "dp")) + (split,) * 6 + (P("dp"), P())
    return jax.shard_map(
        body,
        mesh=mesh,
        in_specs=placed,
        out_specs=(P("dp", "fsdp"),) + (split,) * 4,
        check_vma=False,
    )
```

time: 187 us -> 137 us (0.73)
  Pallas kernels: 176 us -> 127 us
    pallas_call x1, Pallas kernels: 176 us -> 127 us  [fused(): pl.pallas_call(functools.partial(kernel, (n_dp, n_f, cap)), out_shape=(ja...]
where the time goes in v2:
time: 137 us
  Pallas kernels  127 us (93%)
  local copies, waits for them, and re-layouts  7.83 us (6%)
  other arithmetic  1.67 us (1%)
    pallas_call x1, Pallas kernels, fused(): pl.pallas_call(functools.partial(kernel, (n_dp, n_f, cap)), out_shape=(ja...  127 us
    unnamed x23, local copies, waits for them, and re-layouts  7.83 us

profile of v2, /device:TPU:1, one launch (start us, length us, event | category | flops | bytes accessed | tf_op | source)
XLA Modules:
  0.0 137.1 jit_solution(13971681072612464057)
XLA Ops:
  0.6 0.0 copy-start.5
  0.6 0.0 copy-start.6
  0.7 0.6 copy-done.5
  1.3 0.0 copy-done.6
  1.3 0.0 copy-start
  1.3 0.9 copy-done
  2.2 0.0 copy-start.1
  2.2 1.0 copy-done.1
  3.2 0.0 copy-start.2
  3.2 0.8 copy-done.2
  4.0 0.0 copy-start.3
  4.0 0.9 copy-done.3
  5.0 0.0 copy-start.4
  5.0 0.9 copy-done.4
  5.9 126.9 %adapter_step.1 = (bf16[384,256]{1,0:T(8,128)(2,1)S(1)}, f32[128,512]{1,0:T(8,128)S(1)}, f32[128,256]{1,0:T(8,128)S(1)}) custom-call(bf16[384,512]{1,0:T(8,128)(2,1)S(1)} %copy-done.1, bf16[384,256]{1,0:T(8,128)(2,1)S(1)} %copy-done.3, bf16[512,128]{1,0:T(8,128)(2,1)S(1)} %copy-done.4, bf16[128,512]{1,0:T(8,128)(2,1)S(1)} %bitcast.6, ...), custom_call_target="tpu_custom_call" | custom-call | tf_op jit(solution)/shard_map/adapter_step/pallas_call | solution.py:443
  132.8 0.0 copy-start.7
  132.8 0.0 copy-start.8
  132.8 0.9 copy-done.7
  133.7 0.1 copy-done.8
  133.8 0.9 add_multiply_fusion
  134.7 0.0 copy-start.9
  134.7 0.0 copy-start.10
  134.7 0.9 copy-done.9
  135.6 0.1 copy-done.10
  135.7 0.7 add_multiply_fusion.2
  136.4 0.7 copy.17
  (2 shorter events, 0.0 us)
Async XLA Ops:
  0.6 0.7 copy-start.5
  0.6 0.7 copy-start.6
  1.3 0.9 copy-start
  2.2 1.0 copy-start.1
  3.2 0.8 copy-start.2
  4.0 0.9 copy-start.3
  5.0 0.9 copy-start.4
  132.8 1.0 copy-start.7
  132.8 1.0 copy-start.8
  134.7 0.9 copy-start.9
  134.7 1.0 copy-start.10

commit v3 on v2

--- a/solution.py
+++ b/solution.py
@@ -34,9 +34,9 @@
 
 def kernel(
     sizes,
-    x_hbm, g_hbm, w_hbm, d_hbm, u_hbm, member_ref, slot_ref,
-    out_ref, gd_ref, gu_ref,
-    x_ref, g_ref, d_ref, u_ref, wt_all, disp_send, disp_recv,
+    x_hbm, g_hbm, w_hbm, d_hbm, u_hbm, member_hbm, slot_hbm, md_hbm, sd_hbm, mu_hbm, su_hbm,
+    out_ref, md_out, sd_out, mu_out, su_out,
+    x_ref, g_ref, d_ref, u_ref, member_ref, slot_ref, md_ref, sd_ref, mu_ref, su_ref, gd_ref, gu_ref, wt_all, disp_send, disp_recv,
     part_send, part_recv, lr_send, lr_recv, lr_all, ret_send, ret_recv, acc,
     in_sem, ring_r_send, ring_r_recv, ring_l_send, ring_l_recv, sib_send, sib_recv,
     disp_ssem, disp_rsem, part_ssem, part_rsem,
@@ -48,8 +48,8 @@
     rows, slab = x_hbm.shape
     width = g_hbm.shape[1]
     hs, hw = slab // 2, width // 2
-    blocks = member_ref.shape[1]
-    members = slot_ref.shape[1]
+    blocks = member_hbm.shape[1]
+    members = slot_hbm.shape[1]
     chunk = cap * BLK
     depth = w_hbm.shape[0]
     me = lax.axis_index("dp")
@@ -92,7 +92,11 @@
     loads = [
         pltpu.make_async_copy(src, dst, in_sem.at[i])
         for i, (src, dst) in enumerate(
-            [(x_hbm, x_ref), (g_hbm, g_ref), (w_hbm, wt_all.at[z, core, pl.ds(0, depth)]), (d_hbm, d_ref), (u_hbm, u_ref)]
+            [
+                (member_hbm, member_ref), (slot_hbm, slot_ref), (x_hbm, x_ref), (g_hbm, g_ref),
+                (w_hbm, wt_all.at[z, core, pl.ds(0, depth)]), (d_hbm, d_ref), (u_hbm, u_ref),
+                (md_hbm, md_ref), (sd_hbm, sd_ref), (mu_hbm, mu_ref), (su_hbm, su_ref),
+            ]
         )
     ]
     for load in loads:
@@ -105,6 +109,9 @@
     @pl.loop(1, n_f)
     def _(k):
         pl.semaphore_signal(barrier, inc=1, device_id=(me, lax.rem(fs + k, n_f)), device_id_type=MESH)
+
+    for load in loads[:2]:
+        load.wait()
 
     slot_col = to_column(slot_ref[...])
     slots = jnp.sum(
@@ -138,8 +145,50 @@
     wt_all[pl.ds(z, 1), pl.ds(core, 1), pl.ds(depth, 16)] = jnp.broadcast_to(
         tags.astype(f32), (16, 128)
     ).astype(bf16)[None, None]
-    for load in loads:
+    for load in loads[2:7]:
         load.wait()
+
+    pl.semaphore_wait(barrier, n_dp + n_f - 2)
+
+    piece = wt_all.shape[2] // PIECES
+
+    def ring_right(src_z, step, q):
+        block = wt_all.at[src_z, core, pl.ds(pl.multiple_of(q * piece, piece), piece)]
+        at = step * PIECES + q
+        return dp_copy(block, block, ring_r_send, ring_r_recv.at[at], right)
+
+    def ring_left(src_z, step, q):
+        block = wt_all.at[src_z, core, pl.ds(pl.multiple_of(q * piece, piece), piece)]
+        at = step * PIECES + q
+        return dp_copy(block, block, ring_l_send, ring_l_recv.at[at], left)
+
+    def to_sibling(src_z):
+        block = wt_all.at[src_z, core]
+        return dp_copy(block, block, sib_send, sib_recv.at[src_z], sibling)
+
+    def from_sibling(src_z):
+        block = wt_all.at[src_z, 1 - core]
+        return dp_copy(block, block, sib_send, sib_recv.at[src_z], sibling)
+
+    def start_ring():
+        @pl.loop(0, PIECES)
+        def _(q):
+            ring_right(z, 1, q).start()
+            ring_left(z, 1, q).start()
+
+        to_sibling(z).start()
+
+    half_places = n_dp // 2
+
+    def disp_to(i):
+        to, at = receiver(i), i // 2 * 2 + core
+        return dp_copy(disp_send.at[to], disp_recv.at[at], disp_ssem, disp_rsem.at[i // half_places], to)
+
+    def several(buffer, count, send_sem, recv_sem):
+        blocks_of = buffer.at[pl.ds(0, count)]
+        return dp_copy(blocks_of, blocks_of, send_sem, recv_sem, sibling)
+
+    start_ring()
 
     halves = [
         jnp.concatenate([x_ref[:, h * hs:(h + 1) * hs], g_ref[:, h * hw:(h + 1) * hw]], axis=1)
@@ -159,48 +208,6 @@
 
     disp_recv[pl.ds(last, 1)] = disp_send[pl.ds(me, 1)]
 
-    pl.semaphore_wait(barrier, n_dp + n_f - 2)
-
-    piece = wt_all.shape[2] // PIECES
-
-    def ring_right(src_z, step, q):
-        block = wt_all.at[src_z, core, pl.ds(pl.multiple_of(q * piece, piece), piece)]
-        at = step * PIECES + q
-        return dp_copy(block, block, ring_r_send, ring_r_recv.at[at], right)
-
-    def ring_left(src_z, step, q):
-        block = wt_all.at[src_z, core, pl.ds(pl.multiple_of(q * piece, piece), piece)]
-        at = step * PIECES + q
-        return dp_copy(block, block, ring_l_send, ring_l_recv.at[at], left)
-
-    def to_sibling(src_z):
-        block = wt_all.at[src_z, core]
-        return dp_copy(block, block, sib_send, sib_recv.at[src_z], sibling)
-
-    def from_sibling(src_z):
-        block = wt_all.at[src_z, 1 - core]
-        return dp_copy(block, block, sib_send, sib_recv.at[src_z], sibling)
-
-    def start_ring():
-        @pl.loop(0, PIECES)
-        def _(q):
-            ring_right(z, 1, q).start()
-            ring_left(z, 1, q).start()
-
-        to_sibling(z).start()
-
-    half_places = n_dp // 2
-
-    def disp_to(i):
-        to, at = receiver(i), i // 2 * 2 + core
-        return dp_copy(disp_send.at[to], disp_recv.at[at], disp_ssem, disp_rsem.at[i // half_places], to)
-
-    def several(buffer, count, send_sem, recv_sem):
-        blocks_of = buffer.at[pl.ds(0, count)]
-        return dp_copy(blocks_of, blocks_of, send_sem, recv_sem, sibling)
-
-    start_ring()
-
     def part_to(j):
         return f_copy(part_send.at[j], part_recv.at[fs], part_ssem, part_rsem, j)
 
@@ -411,6 +418,17 @@
     give_back(1)
     ret_recv[pl.ds(last, 1)] = ret_send[pl.ds(last, 1)]
     pl.loop(groups, 2 * groups)(gradients)
+
+    for load in loads[7:]:
+        load.wait()
+    for maps, rate, grad, mean, square, new_mean, new_square in (
+        (d_ref, rate_down, gd_ref, md_ref, sd_ref, md_out, sd_out),
+        (u_ref, rate_up, gu_ref, mu_ref, su_ref, mu_out, su_out),
+    ):
+        theta = maps[...].astype(f32) - (rate * adapter_scale) * grad[...]
+        new_mean[...] = (SNAPS * mean[...] + theta) / (SNAPS + 1.0)
+        new_square[...] = (SNAPS * square[...] + theta * theta) / (SNAPS + 1.0)
+
     ret_arrive(0)
     ret_arrive(1)
     out_ref[...] = acc[...].astype(bf16)
@@ -429,7 +447,7 @@
     several(ret_send, n_dp - 1, ret_ssem, ret_rsem.at[0]).wait_send()
 
 
-def fused(x, g, w, down, up, block_member, member_slot):
+def fused(x, g, w, down, up, block_member, member_slot, *moments):
     n_dp, n_f = lax.axis_size("dp"), lax.axis_size("fsdp")
     rows, slab = x.shape
     width = g.shape[1]
@@ -444,14 +462,16 @@
         functools.partial(kernel, (n_dp, n_f, cap)),
         out_shape=(
             jax.ShapeDtypeStruct((rows, width), bf16),
-            jax.ShapeDtypeStruct(down.shape, f32),
-            jax.ShapeDtypeStruct(up.shape, f32),
-        ),
-        in_specs=[hbm] * 5 + [vmem] * 2,
-        out_specs=(vmem,) * 3,
+        )
+        + tuple(jax.ShapeDtypeStruct(moment.shape, f32) for moment in moments),
+        in_specs=[hbm] * 11,
+        out_specs=(vmem,) * 5,
         scratch_shapes=[
             pltpu.VMEM(x.shape, bf16), pltpu.VMEM(g.shape, bf16),
             pltpu.VMEM(down.shape, bf16), pltpu.VMEM(up.shape, bf16),
+            pltpu.VMEM(block_member.shape, jnp.int32), pltpu.VMEM(member_slot.shape, jnp.int32),
+            *(pltpu.VMEM(moment.shape, f32) for moment in moments),
+            pltpu.VMEM(down.shape, f32), pltpu.VMEM(up.shape, f32),
             pltpu.VMEM((n_z, 2, w.shape[0] + 16, 128), bf16),
             pltpu.VMEM((n_dp, 2 * chunk, (slab + width) // 2), bf16),
             pltpu.VMEM((n_dp, 2 * chunk, (slab + width) // 2), bf16),
@@ -463,39 +483,59 @@
             pltpu.VMEM((n_dp, 2 * chunk, width // 2), bf16),
             pltpu.VMEM((n_dp, 2 * chunk, width // 2), bf16),
             pltpu.VMEM((rows, width), f32),
-            dma((5,)), dma, dma((hops,)), dma, dma((hops,)), dma, dma((n_z,)),
+            dma((11,)), dma, dma((hops,)), dma, dma((hops,)), dma, dma((n_z,)),
             dma, dma((2,)), dma, dma, dma, dma, dma, dma((2,)), dma, dma((2,)),
         ],
         compiler_params=pltpu.CompilerParams(
-            collective_id=0, has_side_effects=True, vmem_limit_bytes=40 * 1024 * 1024
+            collective_id=0, has_side_effects=True, vmem_limit_bytes=60 * 1024 * 1024
         ),
         name="adapter_step",
-    )(x, g, w, down, up, block_member, member_slot)
+    )(x, g, w, down, up, block_member, member_slot, *moments)
+
+
+def settle(*results):
+    n = len(results)
+
+    def move(*refs):
+        here, sems = refs[2 * n:3 * n], refs[-1]
+        loads = [pltpu.make_async_copy(refs[i], here[i], sems.at[i]) for i in range(n)]
+        stores = [pltpu.make_async_copy(here[i], refs[n + i], sems.at[n + i]) for i in range(n)]
+        for load in loads:
+            load.start()
+        for load, store in zip(loads, stores):
+            load.wait()
+            store.start()
+        for store in stores:
+            store.wait()
+
+    anywhere = pl.BlockSpec(memory_space=pl.ANY)
+    return pl.pallas_call(
+        move,
+        out_shape=tuple(jax.ShapeDtypeStruct(r.shape, r.dtype) for r in results),
+        in_specs=[anywhere] * n,
+        out_specs=(anywhere,) * n,
+        scratch_shapes=[*(pltpu.VMEM(r.shape, r.dtype) for r in results), pltpu.SemaphoreType.DMA((2 * n,))],
+        name="settle",
+    )(*results)
 
 
 def body(
     inputs, out_grad, base_weight, down_maps, up_maps,
     mean_down, square_down, mean_up, square_up, block_member, member_slot,
 ):
-    owned, rank, slab_width = down_maps.shape
-    out_width = up_maps.shape[2]
-    projected, down_gradient, up_gradient = fused(
-        inputs,
-        out_grad,
-        base_weight,
-        down_maps.reshape(owned * rank, slab_width),
-        up_maps.reshape(owned * rank, out_width),
-        block_member.reshape(1, -1),
-        member_slot.reshape(1, -1),
+    maps = (down_maps, up_maps)
+    moments = (mean_down, square_down, mean_up, square_up)
+
+    def flat(value):
+        return value.reshape(-1, value.shape[2])
+
+    projected, *news = settle(
+        *fused(
+            inputs, out_grad, base_weight, *map(flat, maps),
+            block_member.reshape(1, -1), member_slot.reshape(1, -1), *map(flat, moments),
+        )
     )
-    theta_down = down_maps.astype(f32) - (rate_down * adapter_scale) * down_gradient.reshape(down_maps.shape)
-    theta_up = up_maps.astype(f32) - (rate_up * adapter_scale) * up_gradient.reshape(up_maps.shape)
-    denominator = SNAPS + 1.0
-    new_mean_down = (SNAPS * mean_down + theta_down) / denominator
-    new_square_down = (SNAPS * square_down + theta_down * theta_down) / denominator
-    new_mean_up = (SNAPS * mean_up + theta_up) / denominator
-    new_square_up = (SNAPS * square_up + theta_up * theta_up) / denominator
-    return (projected, new_mean_down, new_square_down, new_mean_up, new_square_up)
+    return (projected, *(new.reshape(old.shape) for new, old in zip(news, moments)))
 
 
 def solution(mesh):

time: 137 us -> 129 us (0.942)
  local copies, waits for them, and re-layouts: 7.83 us -> 0 us
  Pallas kernels: 127 us -> 129 us
  other arithmetic: 1.67 us -> 0 us
    unnamed x23 -> x0, local copies, waits for them, and re-layouts: 7.83 us -> none
    pallas_call x0 -> x1, Pallas kernels: none -> 2.01 us  [settle(): pl.pallas_call(move, out_shape=tuple((jax.ShapeDtypeStruct(r.shape, r.dty...]
    div x2 -> x0, other arithmetic: 1.63 us -> none  [the longest x1 0.89 us: body(): (SNAPS * square_down + theta_down * theta_down) / denominator]
where the time goes in v3:
time: 129 us
  Pallas kernels  129 us (100%)
    pallas_call x1, Pallas kernels, fused(): pl.pallas_call(functools.partial(kernel, (n_dp, n_f, cap)), out_shape=(ja...  127 us

profile of v3, /device:TPU:1, one launch (start us, length us, event | category | flops | bytes accessed | tf_op | source)
XLA Modules:
  0.0 129.2 jit_solution(4577688614549458439)
XLA Ops:
  0.6 126.5 %adapter_step.1 = (bf16[384,256]{1,0:T(8,128)(2,1)}, f32[128,512]{1,0:T(8,128)}, f32[128,512]{1,0:T(8,128)}, f32[128,256]{1,0:T(8,128)}, f32[128,256]{1,0:T(8,128)}) custom-call(bf16[384,512]{1,0:T(8,128)(2,1)} %x_hbm.1, bf16[384,256]{1,0:T(8,128)(2,1)} %g_hbm.1, bf16[512,128]{1,0:T(8,128)(2,1)} %w_hbm.1, bf16[128,512]{1,0:T(8,128)(2,1)} %bitcast.14, ...), custom_call_target="tpu_custom_call" | custom-call | tf_op jit(solution)/shard_map/adapter_step/pallas_call | solution.py:461
  127.2 2.0 %settle.1 = (bf16[384,256]{1,0:T(8,128)(2,1)}, f32[128,512]{1,0:T(8,128)}, f32[128,512]{1,0:T(8,128)}, f32[128,256]{1,0:T(8,128)}, f32[128,256]{1,0:T(8,128)}) custom-call(bf16[384,256]{1,0:T(8,128)(2,1)} %get-tuple-element.15.refs_0_, f32[128,512]{1,0:T(8,128)} %get-tuple-element.16.refs_1_, f32[128,512]{1,0:T(8,128)} %get-tuple-element.17.refs_2_, ...), custom_call_target="tpu_custom_call" | custom-call | tf_op jit(solution)/shard_map/settle/pallas_call | solution.py:512

commit v4 on v3

--- a/solution.py
+++ b/solution.py
@@ -182,7 +182,7 @@
 
     def disp_to(i):
         to, at = receiver(i), i // 2 * 2 + core
-        return dp_copy(disp_send.at[to], disp_recv.at[at], disp_ssem, disp_rsem.at[i // half_places], to)
+        return dp_copy(disp_send.at[to], disp_recv.at[at], disp_ssem, disp_rsem.at[i // GROUP], to)
 
     def several(buffer, count, send_sem, recv_sem):
         blocks_of = buffer.at[pl.ds(0, count)]
@@ -301,7 +301,10 @@
         return f_copy(lr_send.at[j], lr_recv.at[fs], rs_ssem, rs_rsem, j)
 
     def ag_to(j):
-        return f_copy(lr_all.at[fs], lr_all.at[fs], ag_ssem, ag_rsem.at[fs // (n_f // 2)], j)
+        return f_copy(lr_all.at[fs], lr_all.at[fs], ag_ssem, ag_rsem.at[fs], j)
+
+    def ag_from(j):
+        return f_copy(lr_all.at[j], lr_all.at[j], ag_ssem, ag_rsem.at[j], j)
 
     def others(n, mine, act):
         @pl.loop(1, n)
@@ -326,7 +329,7 @@
 
     def ret_to(i):
         to, at = sender(i), i // 2 * 2 + core
-        return dp_copy(ret_send.at[i], ret_recv.at[at], ret_ssem, ret_rsem.at[i // half_places], to)
+        return dp_copy(ret_send.at[i], ret_recv.at[at], ret_ssem, ret_rsem.at[i // GROUP], to)
 
     def adapt(i):
         low, _ = by_slot(ranked(i), got_tags(i))
@@ -346,18 +349,21 @@
         pick = jnp.where(goal == row_target_col, 1.0, 0.0).astype(bf16)
         acc[...] += jnp.dot(pick, value, preferred_element_type=f32)
 
-    def count(half):
-        return half_places - half
-
-    def arrive(half):
-        several(disp_recv, count(half), disp_ssem, disp_rsem.at[half]).wait_recv()
+    def arrived(i, buffer, send_sem, recv_sem):
+        own = i == n_dp // GROUP - 1
+        for is_own in (True, False):
+            @pl.when(own == is_own)
+            def _():
+                several(buffer, GROUP - is_own, send_sem, recv_sem.at[i]).wait_recv()
 
     groups = n_dp // GROUP // 2
 
     def scatter(half):
-        low_j, high_j = half * (n_f // 2), (half + 1) * (n_f // 2)
-        pl.loop(half * groups, (half + 1) * groups)(project)
-        but_me(low_j, high_j, lambda j: rs_to(j).start())
+        @pl.loop(half * groups, (half + 1) * groups)
+        def _(i):
+            arrived(i, disp_recv, disp_ssem, disp_rsem)
+            project(i)
+            but_me(2 * i, 2 * i + 2, lambda j: rs_to(j).start())
 
     def reduce(half):
         @pl.when(fs // (n_f // 2) == half)
@@ -368,14 +374,12 @@
             others(n_f, fs, lambda j: ag_to(j).start())
 
     def give_back(half):
-        mine = fs // (n_f // 2) == half
-        for is_mine, chunks in ((True, n_f // 2 - 1), (False, n_f // 2)):
-            @pl.when(mine == is_mine)
-            def _():
-                several(lr_all, chunks, ag_ssem, ag_rsem.at[half]).wait_recv()
-
-        pl.loop(half * groups, (half + 1) * groups)(adapt)
-        places(half * half_places, (half + 1) * half_places, lambda i: ret_to(i).start())
+        @pl.loop(half * groups, (half + 1) * groups)
+        def _(i):
+            but_me(2 * i, 2 * i + 2, lambda j: ag_from(j).wait_recv())
+            adapt(i)
+            places(i * GROUP, (i + 1) * GROUP, lambda k: ret_to(k).start())
+
 
     def gradients(i):
         got = disp_recv[pl.ds(i * GROUP, GROUP)].reshape(GROUP * 2 * chunk, hs + hw)
@@ -394,18 +398,18 @@
             gu_ref[:, h * hw:(h + 1) * hw] += part(low, h, got[:, hs:])
 
     def ret_arrive(half):
-        several(ret_recv, count(half), ret_ssem, ret_rsem.at[half]).wait_recv()
-        pl.loop(half * groups, (half + 1) * groups)(take)
-
-    arrive(0)
+        @pl.loop(half * groups, (half + 1) * groups)
+        def _(i):
+            arrived(i, ret_recv, ret_ssem, ret_rsem)
+            take(i)
+
     scatter(0)
     reduce(0)
-    give_back(0)
     gd_ref[...] = jnp.zeros_like(gd_ref)
     gu_ref[...] = jnp.zeros_like(gu_ref)
-    arrive(1)
     scatter(1)
-
+    give_back(0)
+    reduce(1)
     several(part_recv, n_f - 1, part_ssem, part_rsem).wait_recv()
     acc[...] = part_recv[0].astype(f32)
 
@@ -413,7 +417,6 @@
     def _(j):
         acc[...] += part_recv[j].astype(f32)
 
-    reduce(1)
     pl.loop(0, groups)(gradients)
     give_back(1)
     ret_recv[pl.ds(last, 1)] = ret_send[pl.ds(last, 1)]
@@ -484,7 +487,7 @@
             pltpu.VMEM((n_dp, 2 * chunk, width // 2), bf16),
             pltpu.VMEM((rows, width), f32),
             dma((11,)), dma, dma((hops,)), dma, dma((hops,)), dma, dma((n_z,)),
-            dma, dma((2,)), dma, dma, dma, dma, dma, dma((2,)), dma, dma((2,)),
+            dma, dma((n_dp // GROUP,)), dma, dma, dma, dma, dma, dma((n_f,)), dma, dma((n_dp // GROUP,)),
         ],
         compiler_params=pltpu.CompilerParams(
             collective_id=0, has_side_effects=True, vmem_limit_bytes=60 * 1024 * 1024

time: 129 us -> 123 us (0.953)
  Pallas kernels: 129 us -> 121 us
    pallas_call x1, Pallas kernels: 127 us -> 119 us  [fused(): pl.pallas_call(functools.partial(kernel, (n_dp, n_f, cap)), out_shape=(ja...]
where the time goes in v4:
time: 123 us; the launch traced here: 122 us
  Pallas kernels  121 us (98%)
    pallas_call x1, Pallas kernels, fused(): pl.pallas_call(functools.partial(kernel, (n_dp, n_f, cap)), out_shape=(ja...  119 us

profile of v4, /device:TPU:1, one launch (start us, length us, event | category | flops | bytes accessed | tf_op | source)
XLA Modules:
  0.0 122.0 jit_solution(463030806837081530)
XLA Ops:
  0.6 119.4 %adapter_step.1 = (bf16[384,256]{1,0:T(8,128)(2,1)}, f32[128,512]{1,0:T(8,128)}, f32[128,512]{1,0:T(8,128)}, f32[128,256]{1,0:T(8,128)}, f32[128,256]{1,0:T(8,128)}) custom-call(bf16[384,512]{1,0:T(8,128)(2,1)} %x_hbm.1, bf16[384,256]{1,0:T(8,128)(2,1)} %g_hbm.1, bf16[512,128]{1,0:T(8,128)(2,1)} %w_hbm.1, bf16[128,512]{1,0:T(8,128)(2,1)} %bitcast.14, ...), custom_call_target="tpu_custom_call" | custom-call | tf_op jit(solution)/shard_map/adapter_step/pallas_call | solution.py:464
  120.0 2.0 %settle.1 = (bf16[384,256]{1,0:T(8,128)(2,1)}, f32[128,512]{1,0:T(8,128)}, f32[128,512]{1,0:T(8,128)}, f32[128,256]{1,0:T(8,128)}, f32[128,256]{1,0:T(8,128)}) custom-call(bf16[384,256]{1,0:T(8,128)(2,1)} %get-tuple-element.15.refs_0_, f32[128,512]{1,0:T(8,128)} %get-tuple-element.16.refs_1_, f32[128,512]{1,0:T(8,128)} %get-tuple-element.17.refs_2_, ...), custom_call_target="tpu_custom_call" | custom-call | tf_op jit(solution)/shard_map/settle/pallas_call | solution.py:515
